TPU v7x, 256 devices: a whole 4x4x8 slice. The times are simulated.
256 devices in a mesh: seq: 64 (over x, z, core), head: 4 (over y).
Axes of the slice: x: 4, y: 4, z: 8, core: 2. Of those that a mesh axis runs over, the one named last changes fastest.
Arguments:
- queries: bfloat16 [8192, 2048], P('seq', 'head'), may hold values from -6 to 6
- key_vecs: bfloat16 [8192, 2048], P('seq', 'head'), may hold values from -6 to 6
- values: bfloat16 [8192, 4096], P('seq', 'head'), may hold values from -6 to 6
- output_gate: bfloat16 [8192, 4096], P('seq', 'head'), may hold values from -6 to 6
- decay_gate: float32 [32, 8192], P('head', 'seq'), may hold values from 0.5 to 1
- write_rate: float32 [32, 8192], P('head', 'seq'), may hold values from 0 to 1
- initial_state: float32 [32, 128, 128], P('head'), may hold values from -0.6 to 0.6
- norm_gain: float32 [128], replicated, may hold values from 0.5 to 1.5
- out_weight: bfloat16 [4096, 2048], P('head'), may hold values from -0.09375 to 0.09375
Outputs:
- layer_out: bfloat16 [8192, 2048], P('seq', 'head')
All inputs are finite; a program needn't handle non-finite values.
Results may differ from a plain program's by a relative error of at most 0.015.
Values may be sent and summed in bfloat16 or wider, within the bound.
A program may use at most 192 MiB of HBM per device.

v0:
```python
import jax
import jax.numpy as jnp
from jax import lax
from jax.sharding import PartitionSpec as P

VALUE_HEADS = 32
HK = 16
STRETCH = 128


HIGH = lax.Precision.HIGHEST


def carried_in(value, axis, join, neutral):
    count, mine = (lax.axis_size(axis), lax.axis_index(axis))
    pieces = jax.tree.map(lambda part: lax.all_gather(part, axis), value)
    so_far = jax.tree.map(
        lambda part, zero: jnp.full_like(part, 0) + jnp.asarray(zero, part.dtype), value, neutral
    )

    def hop(position, so_far):
        longer = join(so_far, jax.tree.map(lambda part: part[position], pieces))
        return jax.tree.map(lambda new, old: jnp.where(position < mine, new, old), longer, so_far)

    return lax.fori_loop(0, count - 1, hop, so_far)


def unit_heads(block, heads):
    rows = block.astype(jnp.float32).reshape(block.shape[0], heads, -1).transpose(1, 0, 2)
    return rows / jnp.sqrt(jnp.sum(rows * rows, axis=-1, keepdims=True) + 1e-06)


def stretch_terms(query_unit, key_unit, vals, logs, rates):
    size = logs.shape[-1]
    width = key_unit.shape[-1]
    row_ids = lax.broadcasted_iota(jnp.int32, (size, size), 0)
    column_index = lax.broadcasted_iota(jnp.int32, (size, size), 1)
    strict = row_ids > column_index
    within = row_ids >= column_index
    lower_ones = within.astype(logs.dtype)
    cum = jnp.einsum("...j,ij->...i", logs, lower_ones, precision=HIGH)
    diff = cum[..., :, None] - cum[..., None, :]
    weighted = key_unit * rates[..., None]
    inner = jnp.einsum("...id,...jd->...ij", weighted, key_unit, precision=HIGH)
    lower_part = jnp.where(strict, inner * jnp.exp(jnp.where(strict, diff, 0.0)), 0.0)
    system = lower_part + jnp.eye(size, dtype=logs.dtype)
    right = jnp.concatenate([weighted * jnp.exp(cum)[..., None], vals * rates[..., None]], axis=-1)
    solved = jax.scipy.linalg.solve_triangular(system, right, lower=True, unit_diagonal=True)
    w_part = solved[..., :width]
    u_part = solved[..., width:]
    scaled_q = query_unit * width ** (-0.5)
    scores = jnp.einsum("...id,...jd->...ij", scaled_q, key_unit, precision=HIGH)
    scores = jnp.where(within, scores * jnp.exp(jnp.where(within, diff, 0.0)), 0.0)
    readout = scaled_q * jnp.exp(cum)[..., None] - jnp.einsum(
        "...ij,...jd->...id", scores, w_part, precision=HIGH
    )
    local_out = jnp.einsum("...ij,...je->...ie", scores, u_part, precision=HIGH)
    last = cum[..., -1]
    carried = key_unit * jnp.exp(last[..., None] - cum)[..., None]
    trans = jnp.exp(last)[..., None, None] * jnp.eye(width, dtype=logs.dtype) - jnp.einsum(
        "...id,...ie->...de", carried, w_part, precision=HIGH
    )
    bias = jnp.einsum("...id,...ie->...de", carried, u_part, precision=HIGH)
    return (readout, local_out, trans, bias)


def gated_norm(out, gate_rows, norm_gain):
    heads = out.shape[0]
    mixed = out.transpose(1, 0, 2)
    scaled = mixed / jnp.sqrt(jnp.mean(mixed * mixed, axis=-1, keepdims=True) + 1e-06) * norm_gain
    gate_vals = gate_rows.astype(jnp.float32).reshape(gate_rows.shape[0], heads, -1)
    return (scaled * jax.nn.silu(gate_vals)).reshape(gate_rows.shape[0], -1).astype(jnp.bfloat16)


def compose(left, right):
    return jnp.einsum("hde,hef->hdf", left, right, precision=HIGH)


def combine(earlier, later):
    return (compose(later[0], earlier[0]), compose(later[0], earlier[1]) + later[1])


def on_device(
    queries,
    key_vecs,
    values,
    output_gate,
    decay_gate,
    write_rate,
    initial_state,
    norm_gain,
    out_weight,
):
    tokens = queries.shape[0]
    local_heads = decay_gate.shape[0]
    group = VALUE_HEADS // HK
    key_heads = local_heads // group
    count = tokens // STRETCH
    width = values.shape[1] // local_heads
    query_unit = jnp.repeat(unit_heads(queries, key_heads), group, axis=0).reshape(
        local_heads, count, STRETCH, -1
    )
    key_unit = jnp.repeat(unit_heads(key_vecs, key_heads), group, axis=0).reshape(
        local_heads, count, STRETCH, -1
    )
    vals = (
        values.astype(jnp.float32)
        .reshape(tokens, local_heads, width)
        .transpose(1, 0, 2)
        .reshape(local_heads, count, STRETCH, width)
    )
    logs = jnp.log(decay_gate).reshape(local_heads, count, STRETCH)
    rates = write_rate.reshape(local_heads, count, STRETCH)
    readout, local_out, trans, bias = stretch_terms(query_unit, key_unit, vals, logs, rates)
    size = trans.shape[-1]
    identity_map = jnp.broadcast_to(jnp.eye(size, dtype=jnp.float32), (local_heads, size, size))
    empty_bias = jnp.zeros_like(initial_state)
    total_trans = identity_map
    total_bias = empty_bias
    position = 0
    total_trans, total_bias = combine(
        (total_trans, total_bias), (trans[:, position], bias[:, position])
    )
    before_trans, before_bias = carried_in(
        (total_trans, total_bias), "seq", combine, (identity_map, empty_bias)
    )
    state = compose(before_trans, initial_state) + before_bias
    position = 0
    pieces = [compose(readout[:, position], state) + local_out[:, position]]
    out = jnp.stack(pieces, axis=1).reshape(local_heads, tokens, width)
    normalized_rows = gated_norm(out, output_gate, norm_gain)
    summed = lax.psum_scatter(
        lax.dot_general(
            out_weight,
            normalized_rows,
            (((0,), (1,)), ((), ())),
            preferred_element_type=jnp.float32,
        ).astype(jnp.bfloat16),
        "head",
        scatter_dimension=0,
        tiled=True,
    ).astype(jnp.float32)
    return summed.T.astype(jnp.bfloat16)


def solution(mesh):
    return jax.shard_map(
        on_device,
        mesh=mesh,
        in_specs=(
            P("seq", "head"),
            P("seq", "head"),
            P("seq", "head"),
            P("seq", "head"),
            P("head", "seq"),
            P("head", "seq"),
            P("head", None, None),
            P(),
            P("head", None),
        ),
        out_specs=P("seq", "head"),
        check_vma=False,
    )
```

profile of v0, /device:TPU:199, one launch (start us, length us, event | category | flops | bytes accessed | tf_op | source)
XLA Modules:
  0.0 650.8 jit_solution(17986691862300150296)
XLA Ops:
  9.4 2.0 fusion.17
  11.4 78.6 %custom-call.4 = f32[8,1,128,128]{2,3,1,0:T(8,128)S(1)} custom-call(f32[8,1,128,128]{3,2,1,0:T(8,128)S(1)} %fusion.17), custom_call_target="InvertDiagBlocksLowerTriangular" | custom-call | tf_op jit(solution)/shard_map/jit(_solve_triangular)/vmap()/triangular_solve | solution.py:48
  95.9 2.0 convolution_add_fusion.3
  101.1 1.9 copy.37
  105.9 132.0 %all-gather.7.cloned.1.call-done = f32[512,128,128]{2,1,0:T(8,128)} async-done(((f32[8,128,128]{2,1,0:T(8,128)}), f32[512,128,128]{2,1,0:T(8,128)}) %all-gather.7.cloned.1.call-update) | async-done | bytes 33554448 | tf_op jit(solution)/shard_map/all_gather | solution.py:16
  237.9 142.3 %all-gather.5.cloned.1.call-done = f32[512,128,128]{2,1,0:T(8,128)} async-done(((f32[8,128,128]{2,1,0:T(8,128)}), f32[512,128,128]{2,1,0:T(8,128)}) %all-gather.5.cloned.1.call-update) | async-done | bytes 33554448 | tf_op jit(solution)/shard_map/all_gather | solution.py:16
  380.2 232.4 %while.16 = (s32[]{:T(128)}, f32[8,128,128]{2,1,0:T(8,128)S(1)}, f32[8,128,128]{2,1,0:T(8,128)S(1)}, s32[]{:T(128)}, f32[64,8,128,128]{3,2,1,0:T(8,128)}, /*index=5*/f32[64,8,128,128]{3,2,1,0:T(8,128)}, s32[]{:T(128)}, s32[]{:T(128)}) while((s32[]{:T(128)}, f32[8,128,128]{2,1,0:T(8,128)S(1)}, f32[8,128,128]{2,1,0:T(8,128)S(1)}, ...), condition=%wide.region_3.4_spmd.clone, body=%wide.region_2.3_spmd.clone.sunk | while | flops 403308544 | bytes 6818920 | solution.py:25
  380.3 1.9 fusion.68
  384.0 1.9 fusion.68
  387.7 1.9 fusion.68
  395.1 1.9 fusion.68
  398.7 1.9 fusion.68
  402.4 1.9 fusion.68
  406.1 1.9 fusion.68
  409.8 1.9 fusion.68
  413.5 1.9 fusion.68
  420.9 1.9 fusion.68
  424.6 1.9 fusion.68
  428.3 1.9 fusion.68
  431.9 1.9 fusion.68
  435.6 1.9 fusion.68
  439.3 1.9 fusion.68
  443.0 1.9 fusion.68
  446.7 1.9 fusion.68
  450.4 1.9 fusion.68
  454.1 1.9 fusion.68
  457.8 1.9 fusion.68
  461.4 1.9 fusion.68
  468.8 1.9 fusion.68
  472.5 1.9 fusion.68
  476.2 1.9 fusion.68
  479.9 1.9 fusion.68
  487.3 1.9 fusion.68
  491.0 1.9 fusion.68
  494.6 1.9 fusion.68
  498.3 1.9 fusion.68
  502.0 1.9 fusion.68
  505.7 1.9 fusion.68
  509.4 1.9 fusion.68
  513.1 1.9 fusion.68
  516.8 1.9 fusion.68
  520.5 1.9 fusion.68
  524.1 1.9 fusion.68
  527.8 1.9 fusion.68
  535.2 1.9 fusion.68
  613.3 2.0 fusion.44
  617.6 3.7 fusion.11
  621.4 22.9 %reduce-scatter.2.cloned.1.call-done = bf16[512,128]{0,1:T(8,128)(2,1)} async-done(((bf16[2048,128]{0,1:T(8,128)(2,1)}), bf16[512,128]{0,1:T(8,128)(2,1)}) %reduce-scatter.2.cloned.1.call-update) | async-done | bytes 131088 | tf_op jit(solution)/shard_map/reduce_scatter | solution.py:132
  (260 shorter events, 175.5 us)
Async XLA Ops:
  6.5 606.1 %copy-start = (f32[8,128,128]{2,1,0:T(8,128)S(1)}, f32[8,128,128]{2,1,0:T(8,128)}, u32[]{:S(2)}) copy-start(f32[8,128,128]{2,1,0:T(8,128)} %param.17) | copy-start | bytes 1572868
  6.5 609.8 %copy-start.1 = (f32[128]{0:T(128)S(1)}, f32[128]{0:T(128)}, u32[]{:S(2)}) copy-start(f32[128]{0:T(128)} %param.18) | copy-start | bytes 1540
  6.5 231.4 %all-gather.7.cloned.1.call-start = ((), (), s32[]{:S(2)}) async-start(), calls=%async_computation.3 | async-start | bytes 34078720 | tf_op jit(solution)/shard_map/all_gather | solution.py:16
  98.0 282.2 %all-gather.5.cloned.1.call-start = ((), (), s32[]{:S(2)}) async-start(), calls=%async_computation.2 | async-start | bytes 34078720 | tf_op jit(solution)/shard_map/all_gather | solution.py:16
  99.4 544.8 %reduce-scatter.2.cloned.1.call-start = ((), (), s32[]{:S(2)}) async-start(), calls=%async_computation.1 | async-start | bytes 655360 | tf_op jit(solution)/shard_map/reduce_scatter | solution.py:132
Sparse Core Ops, SparseCore 0:
  98.1 139.8 all-gather.6
  240.7 139.4 all-gather.4
  621.5 22.7 reduce-scatter.1
where the time goes:
time: 660 us; the launch traced here: 651 us
  waiting for transfers between devices  297 us (45%)
  matrix products  244 us (37%)
  other arithmetic  83 us (13%)
  between operations  13.4 us (2%)
  local copies, waits for them, and re-layouts  10 us (2%)
    all_gather x2, waiting for transfers between devices, carried_in(): pieces = jax.tree.map(lambda part: lax.all_gather(part, axis), value)  274 us
    dot_general x130, matrix products, compose(): return jnp.einsum('hde,hef->hdf', left, right, precision=HIGH)  229 us
    another operation x2, other arithmetic, stretch_terms(): jax.scipy.linalg.solve_triangular(system, right, lower=True, unit_diagona...  78.6 us
    reduce_scatter x1, waiting for transfers between devices, on_device(): lax.psum_scatter(lax.dot_general(out_weight, normalized_rows, (((0,), (1,...  22.9 us
  transfers between devices with their start and end apart: 3, of which 3 were waited for; matrix products, arithmetic and copies ran while one was open for 1% of the time, Pallas kernels for 0%

commit v1 on v0

v1 whole, which is shorter than its diff:
```python
import functools

import jax
import jax.numpy as jnp
from jax import lax
from jax.experimental import pallas as pl
from jax.experimental.pallas import tpu as pltpu
from jax.sharding import PartitionSpec as P

MESH = pl.DeviceIdType.MESH
F32 = jnp.float32
BF16 = jnp.bfloat16
HEADS = 8
KEYS = 4
C = 128
NX = 4
NZ = 8
NY = 4
HALF = HEADS // 2
MSG = 2 * C + 16
OUT = 512


def mm(a, b):
    return lax.dot_general(a, b, (((1,), (0,)), ((), ())), preferred_element_type=F32)


def mm_t(a, b):
    return lax.dot_general(a, b, (((1,), (1,)), ((), ())), preferred_element_type=F32)


def put_gain(ref, index, gain):
    wide = jnp.broadcast_to(gain, (8, C))
    high = wide.astype(BF16).astype(F32)
    ref[index, 2 * C :, :] = jnp.concatenate([high, wide - high], axis=0).astype(BF16)


def get_gain(ref, index):
    rows = ref[index, 2 * C :, :].astype(F32)
    return rows[0:1, :] + rows[8:9, :]


def kernel(
    q_ref,
    k_ref,
    v_ref,
    gate_hbm,
    decay_ref,
    rate_ref,
    init_hbm,
    gain_ref,
    weight_hbm,
    out_ref,
    gate_ref,
    init_ref,
    weight_ref,
    wu_ref,
    score_ref,
    read_ref,
    local_ref,
    silu_ref,
    own,
    sib,
    comb,
    chain,
    total,
    prefix_d,
    prefix_c,
    prefix_g,
    state,
    give,
    take,
    normed,
    part,
    parts,
    load_sem,
    sib_send,
    sib_recv,
    comb_send,
    chain_recv,
    total_send,
    total_recv,
    give_send,
    take_recv,
    part_send,
    parts_recv,
):
    seq, y = lax.axis_index("seq"), lax.axis_index("head")
    x, z, c = seq // 16, lax.rem(seq // 2, NZ), lax.rem(seq, 2)
    base = x * 16
    other = base + z * 2 + (1 - c)

    def remote(src, dst, send, recv, to_seq, to_y):
        return pltpu.make_async_remote_copy(
            src_ref=src,
            dst_ref=dst,
            send_sem=send,
            recv_sem=recv,
            device_id=(to_seq, to_y),
            device_id_type=MESH,
        )

    barrier = pltpu.get_barrier_semaphore()
    for step in range(1, 16):
        pl.semaphore_signal(
            barrier, inc=1, device_id=(base + lax.rem(z * 2 + c + step, 16), y), device_id_type=MESH
        )
    for step in range(1, NX):
        pl.semaphore_signal(
            barrier, inc=1, device_id=(lax.rem(seq + 16 * step, 64), y), device_id_type=MESH
        )
    for step in range(1, NY):
        pl.semaphore_signal(
            barrier, inc=1, device_id=(seq, lax.rem(y + step, NY)), device_id_type=MESH
        )
    loads = [
        pltpu.make_async_copy(init_hbm, init_ref, load_sem.at[0]),
        pltpu.make_async_copy(gate_hbm, gate_ref, load_sem.at[1]),
        pltpu.make_async_copy(weight_hbm, weight_ref, load_sem.at[2]),
    ]
    for load in loads:
        load.start()

    rows = lax.broadcasted_iota(jnp.int32, (C, C), 0)
    cols = lax.broadcasted_iota(jnp.int32, (C, C), 1)
    apart = rows ^ cols
    strict = rows > cols
    within = rows >= cols
    diagonal = (rows == cols).astype(F32)
    upto = (rows <= cols).astype(BF16)
    logs = jnp.log(decay_ref[...])
    rates = rate_ref[...]
    high = logs.astype(BF16)
    rest = logs - high.astype(F32)
    middle = rest.astype(BF16)
    low = (rest - middle.astype(F32)).astype(BF16)
    cum = mm(high, upto) + (mm(middle, upto) + mm(low, upto))
    tall = jnp.concatenate([cum, rates, jnp.zeros((C - 2 * HEADS, C), F32)], axis=0).T
    ends = [cum[h : h + 1, C - 1 : C] for h in range(HEADS)]

    lower, inverse, row_keys, col_keys = [], [], [], []
    for kh in range(KEYS):
        keys = k_ref[:, kh * C : (kh + 1) * C]
        asks = q_ref[:, kh * C : (kh + 1) * C]
        inner = mm_t(keys, keys)
        cross = mm_t(asks, keys)
        squares = inner * diagonal
        row_key = lax.rsqrt(jnp.sum(squares, axis=0, keepdims=True) + 1e-6)
        col_key = lax.rsqrt(jnp.sum(squares, axis=1, keepdims=True) + 1e-6)
        wide_asks = asks.astype(F32)
        col_ask = lax.rsqrt(jnp.sum(wide_asks * wide_asks, axis=1, keepdims=True) + 1e-6)
        col_ask = col_ask * (C**-0.5)
        row_keys.append(row_key)
        col_keys.append(col_key)
        for h in (2 * kh, 2 * kh + 1):
            cum_col = tall[:, h : h + 1]
            rate_col = tall[:, HEADS + h : HEADS + h + 1]
            fade = jnp.exp(jnp.where(within, cum_col - cum[h : h + 1, :], 0.0))
            fade = fade * row_key
            low_part = jnp.where(strict, inner * fade * (rate_col * col_key), 0.0).astype(BF16)
            lower.append(low_part)
            score_ref[h] = jnp.where(within, cross * fade * col_ask, 0.0).astype(BF16)
            read_ref[h] = wide_asks * (col_ask * jnp.exp(cum_col))
            inverse.append(jnp.where(apart == 1, -low_part.astype(F32), diagonal).astype(BF16))
    size = 2
    while size < C:
        mask = ((apart >= size) & (apart < 2 * size)).astype(BF16)
        firsts = [mm(inverse[h], lower[h] * mask).astype(BF16) for h in range(HEADS)]
        inverse = [inverse[h] - mm(firsts[h], inverse[h]).astype(BF16) for h in range(HEADS)]
        size *= 2
    for kh in range(KEYS):
        keys = k_ref[:, kh * C : (kh + 1) * C]
        keys_t = keys.astype(F32).T.astype(BF16)
        for h in (2 * kh, 2 * kh + 1):
            wide = inverse[h].astype(F32)
            rate_row = rates[h : h + 1, :]
            cum_row = cum[h : h + 1, :]
            w_part = mm((wide * (rate_row * jnp.exp(cum_row) * row_keys[kh])).astype(BF16), keys)
            u_part = mm((wide * rate_row).astype(BF16), v_ref[:, h * C : (h + 1) * C])
            both = jnp.concatenate([w_part, u_part], axis=1)
            wu_ref[h] = both.astype(BF16)
            fade_col = col_keys[kh] * jnp.exp(ends[h] - tall[:, h : h + 1])
            maps = mm(keys_t, (both * fade_col).astype(BF16))
            own[h, 0:C, :] = maps[:, 0:C].astype(BF16)
            own[h, C : 2 * C, :] = maps[:, C:].astype(BF16)
            put_gain(own, h, jnp.exp(ends[h]))

    pl.semaphore_wait(barrier, 15 + NX - 1 + NY - 1)

    to_other = [
        remote(own.at[h], sib.at[h], sib_send.at[h], sib_recv.at[h], other, y)
        for h in range(HEADS)
    ]

    @pl.when(c == 0)
    def _():
        for h in range(HALF, HEADS):
            to_other[h].start()

    for h in range(HALF):
        to_other[h].start()

    def joined(index):
        h = c * HALF + index
        remote(own.at[h], sib.at[h], sib_send.at[h], sib_recv.at[h], other, y).wait_recv()
        mine, theirs = own[h, 0 : 2 * C, :], sib[h, 0 : 2 * C, :]
        my_gain, their_gain = get_gain(own, h), get_gain(sib, h)
        first = c == 0
        early = jnp.where(first, mine.astype(F32), theirs.astype(F32))
        late = jnp.where(first, theirs.astype(F32), mine.astype(F32))
        early_gain = jnp.where(first, my_gain, their_gain)
        late_gain = jnp.where(first, their_gain, my_gain)
        late_map = late[0:C].astype(BF16)
        pair = jnp.concatenate([early[0:C], early[C:]], axis=1).astype(BF16)
        moved = mm(late_map, pair)
        comb[index, 0:C, :] = (
            late_gain * early[0:C] + early_gain * late[0:C] - moved[:, 0:C]
        ).astype(BF16)
        comb[index, C : 2 * C, :] = (late_gain * early[C:] + late[C:] - moved[:, C:]).astype(BF16)
        put_gain(comb, index, early_gain * late_gain)

    def to_chain(index):
        h = c * HALF + index
        return remote(
            comb.at[index],
            chain.at[z],
            comb_send.at[index],
            chain_recv.at[z],
            base + h * 2 + c,
            y,
        )

    for index in range(HALF):
        joined(index)

        @pl.when(z != c * HALF + index)
        def _():
            to_chain(index).start()

        @pl.when(z == c * HALF + index)
        def _():
            chain[z] = comb[index]

    for h in range(HEADS):
        pair = mm(score_ref[h], wu_ref[h])
        read_ref[h] = read_ref[h] - pair[:, 0:C]
        local_ref[h] = pair[:, C:]
    loads[1].wait()
    gate = gate_ref[...].astype(F32)
    gains = jnp.concatenate([gain_ref[...]] * HEADS, axis=1)
    silu_ref[...] = gate / (1.0 + jnp.exp(-gate)) * gains
    loads[0].wait()
    loads[2].wait()

    works = z // HALF == c

    def to_segment(step):
        return remote(
            total.at[x],
            total.at[x],
            total_send.at[step],
            total_recv.at[x],
            lax.rem(seq + 16 * step, 64),
            y,
        )

    def to_chip(j, core):
        return remote(
            give.at[j],
            take.at[z],
            give_send.at[j * 2 + core],
            take_recv.at[z],
            base + j * 2 + core,
            y,
        )

    @pl.when(works)
    def _():
        d_now = jnp.zeros((C, C), F32)
        c_now = jnp.zeros((C, C), F32)
        g_now = jnp.ones((1, C), F32)
        for j in range(NZ):

            @pl.when(z != j)
            def _():
                remote(
                    chain.at[j], chain.at[j], comb_send.at[0], chain_recv.at[j], other, y
                ).wait_recv()

            prefix_d[j] = d_now.astype(BF16)
            prefix_c[j] = c_now
            prefix_g[j] = jnp.broadcast_to(g_now, (8, C))
            step_map = chain[j, 0:C, :]
            step_bias = chain[j, C : 2 * C, :].astype(F32)
            gain = get_gain(chain, j)
            wide_map = step_map.astype(F32)
            if j == 0:
                d_now, c_now = wide_map, step_bias
            else:
                moved = mm(step_map, jnp.concatenate([d_now, c_now], axis=1).astype(BF16))
                d_now = gain * d_now + g_now * wide_map - moved[:, 0:C]
                c_now = gain * c_now + step_bias - moved[:, C:]
            g_now = g_now * gain
        total[x, 0:C, :] = d_now.astype(BF16)
        total[x, C : 2 * C, :] = c_now.astype(BF16)
        put_gain(total, x, g_now)
        for step in range(1, NX):

            @pl.when(x + step < NX)
            def _():
                to_segment(step).start()

        state[...] = init_ref[z]
        for before in range(NX - 1):

            @pl.when(before < x)
            def _():
                remote(
                    total.at[before],
                    total.at[before],
                    total_send.at[0],
                    total_recv.at[before],
                    other,
                    y,
                ).wait_recv()
                now = state[...]
                state[...] = (
                    get_gain(total, before) * now
                    - mm(total[before, 0:C, :], now.astype(BF16))
                    + total[before, C : 2 * C, :].astype(F32)
                )

        entry = state[...]
        narrow = entry.astype(BF16)
        for j in range(NZ):
            here = prefix_g[j][0:1, :] * entry - mm(prefix_d[j], narrow) + prefix_c[j]
            give[j] = here.astype(BF16)
            for core in range(2):

                @pl.when((z != j) | (c != core))
                def _():
                    to_chip(j, core).start()

        take[z] = give[z]

    @pl.when(c == 1)
    def _():
        for h in range(HALF):
            to_other[h].wait_recv()

    for h in range(HEADS):

        @pl.when(jnp.logical_not(works) | (z != h))
        def _():
            remote(take.at[h], take.at[h], give_send.at[0], take_recv.at[h], other, y).wait_recv()

        @pl.when(c == 1)
        def _():
            now = take[h]
            here = (
                get_gain(sib, h) * now.astype(F32)
                - mm(sib[h, 0:C, :], now)
                + sib[h, C : 2 * C, :].astype(F32)
            )
            take[h] = here.astype(BF16)

        o = mm(read_ref[h].astype(BF16), take[h]) + local_ref[h]
        scale = lax.rsqrt(jnp.sum(o * o, axis=1, keepdims=True) * (1.0 / C) + 1e-6)
        normed[:, h * C : (h + 1) * C] = (o * scale * silu_ref[:, h * C : (h + 1) * C]).astype(BF16)

    def columns(to_y):
        return weight_ref[:, pl.ds(pl.multiple_of(to_y * OUT, OUT), OUT)]

    def to_row(step):
        return remote(
            part.at[step],
            parts.at[step],
            part_send.at[step],
            parts_recv.at[step],
            seq,
            lax.rem(y + step, NY),
        )

    for step in (2, 1, 3):
        part[step] = mm(normed[...], columns(lax.rem(y + step, NY))).astype(BF16)
        to_row(step).start()
    mine = mm(normed[...], columns(y))
    for step in (1, 3, 2):
        to_row(step).wait_recv()
        mine = mine + parts[step].astype(F32)
    out_ref[...] = mine.astype(BF16)

    for step in (2, 1, 3):
        to_row(step).wait_send()
    for h in range(HALF):
        to_other[h].wait_send()

    @pl.when(c == 0)
    def _():
        for h in range(HALF, HEADS):
            to_other[h].wait_send()

    for index in range(HALF):

        @pl.when(z != c * HALF + index)
        def _():
            to_chain(index).wait_send()

    @pl.when(works)
    def _():
        for step in range(1, NX):

            @pl.when(x + step < NX)
            def _():
                to_segment(step).wait_send()

        for j in range(NZ):
            for core in range(2):

                @pl.when((z != j) | (c != core))
                def _():
                    to_chip(j, core).wait_send()


def on_device(q, k, v, gate, decay, rate, init, gain, weight):
    vmem = pl.BlockSpec(memory_space=pltpu.VMEM)
    anywhere = pl.BlockSpec(memory_space=pl.ANY)
    dma = pltpu.SemaphoreType.DMA
    return pl.pallas_call(
        kernel,
        out_shape=jax.ShapeDtypeStruct((C, OUT), BF16),
        in_specs=[vmem, vmem, vmem, anywhere, vmem, vmem, anywhere, vmem, anywhere],
        out_specs=vmem,
        scratch_shapes=[
            pltpu.VMEM((C, HEADS * C), BF16),
            pltpu.VMEM((HEADS, C, C), F32),
            pltpu.VMEM((HEADS * C, NY * OUT), BF16),
            pltpu.VMEM((HEADS, C, 2 * C), BF16),
            pltpu.VMEM((HEADS, C, C), BF16),
            pltpu.VMEM((HEADS, C, C), F32),
            pltpu.VMEM((HEADS, C, C), F32),
            pltpu.VMEM((C, HEADS * C), F32),
            pltpu.VMEM((HEADS, MSG, C), BF16),
            pltpu.VMEM((HEADS, MSG, C), BF16),
            pltpu.VMEM((HALF, MSG, C), BF16),
            pltpu.VMEM((NZ, MSG, C), BF16),
            pltpu.VMEM((NX, MSG, C), BF16),
            pltpu.VMEM((NZ, C, C), BF16),
            pltpu.VMEM((NZ, C, C), F32),
            pltpu.VMEM((NZ, 8, C), F32),
            pltpu.VMEM((C, C), F32),
            pltpu.VMEM((NZ, C, C), BF16),
            pltpu.VMEM((HEADS, C, C), BF16),
            pltpu.VMEM((C, HEADS * C), BF16),
            pltpu.VMEM((NY, C, OUT), BF16),
            pltpu.VMEM((NY, C, OUT), BF16),
            dma((3,)),
            dma((HEADS,)),
            dma((HEADS,)),
            dma((HALF,)),
            dma((NZ,)),
            dma((NX,)),
            dma((NX,)),
            dma((2 * NZ,)),
            dma((HEADS,)),
            dma((NY,)),
            dma((NY,)),
        ],
        compiler_params=pltpu.CompilerParams(
            collective_id=0, has_side_effects=True, vmem_limit_bytes=40 * 2**20
        ),
        cost_estimate=pl.CostEstimate(
            flops=2 * 10**9, bytes_accessed=6 * 10**6, transcendentals=10**6
        ),
    )(q, k, v, gate, decay, rate, init, gain.reshape(1, C), weight)


def solution(mesh):
    return jax.shard_map(
        on_device,
        mesh=mesh,
        in_specs=(
            P("seq", "head"),
            P("seq", "head"),
            P("seq", "head"),
            P("seq", "head"),
            P("head", "seq"),
            P("head", "seq"),
            P("head", None, None),
            P(),
            P("head", None),
        ),
        out_specs=P("seq", "head"),
        check_vma=False,
    )
```

time: 660 us -> 51.5 us (0.08); the launches traced: 651 us -> 51.2 us
  waiting for transfers between devices: 297 us -> 0 us
  matrix products: 244 us -> 0 us
  other arithmetic: 83 us -> 0 us
  Pallas kernels: 0 us -> 41.5 us
  between operations: 13.4 us -> 0.02 us
    all_gather x2 -> x0, waiting for transfers between devices: 274 us -> none  [carried_in(): pieces = jax.tree.map(lambda part: lax.all_gather(part, axis), value)]
    dot_general x138 -> x0, matrix products: 242 us -> none  [the longest x130 229 us: compose(): return jnp.einsum('hde,hef->hdf', left, right, precision=HIGH)]
    another operation x2 -> x0, other arithmetic: 78.6 us -> none  [stretch_terms(): jax.scipy.linalg.solve_triangular(system, right, lower=True, unit_diagona...]
    pallas_call x0 -> x1, Pallas kernels: none -> 41.5 us  [on_device(): pl.pallas_call(kernel, out_shape=jax.ShapeDtypeStruct((C, OUT), BF16), in...]
    reduce_scatter x1 -> x0, waiting for transfers between devices: 22.9 us -> none  [on_device(): lax.psum_scatter(lax.dot_general(out_weight, normalized_rows, (((0,), (1,...]
    unnamed x5 -> x19, local copies, waits for them, and re-layouts: 1.13 us -> 9.62 us
  transfers between devices with their start and end apart: 3 -> 0, of which waited for: 3 -> 0; matrix products, arithmetic and copies ran while one was open for 1% -> 0% of each run, Pallas kernels for 0% -> 0%
where the time goes in v1:
time: 51.5 us; the launch traced here: 51.2 us
  Pallas kernels  41.5 us (81%)
  local copies, waits for them, and re-layouts  9.62 us (19%)
    pallas_call x1, Pallas kernels, on_device(): pl.pallas_call(kernel, out_shape=jax.ShapeDtypeStruct((C, OUT), BF16), in...  41.5 us
    unnamed x19, local copies, waits for them, and re-layouts  9.62 us

profile of v1, /device:TPU:199, one launch (start us, length us, event | category | flops | bytes accessed | tf_op | source)
XLA Modules:
  0.0 51.2 jit_solution(9176635454358229019)
XLA Ops:
  0.0 0.0 copy-start
  0.0 2.2 %copy-done = bf16[1024,2048]{1,0:T(8,128)(2,1)S(1)} copy-done((bf16[1024,2048]{1,0:T(8,128)(2,1)S(1)}, bf16[1024,2048]{1,0:T(8,128)(2,1)}, u32[]{:S(2)}) %copy-start) | copy-done | bytes 4194328
  2.2 0.0 copy-start.1
  2.2 1.0 %copy-done.1 = f32[8,128,128]{2,1,0:T(8,128)S(1)} copy-done((f32[8,128,128]{2,1,0:T(8,128)S(1)}, f32[8,128,128]{2,1,0:T(8,128)}, u32[]{:S(2)}) %copy-start.1) | copy-done | bytes 524312
  3.2 0.0 copy-start.2
  3.2 0.9 %copy-done.2 = bf16[128,1024]{1,0:T(8,128)(2,1)S(1)} copy-done((bf16[128,1024]{1,0:T(8,128)(2,1)S(1)}, bf16[128,1024]{1,0:T(8,128)(2,1)}, u32[]{:S(2)}) %copy-start.2) | copy-done | bytes 262168
  4.2 0.0 copy-start.3
  4.2 0.9 %copy-done.3 = bf16[128,1024]{1,0:T(8,128)(2,1)S(1)} copy-done((bf16[128,1024]{1,0:T(8,128)(2,1)S(1)}, bf16[128,1024]{1,0:T(8,128)(2,1)}, u32[]{:S(2)}) %copy-start.3) | copy-done | bytes 262168
  5.1 0.0 copy-start.4
  5.1 0.9 %copy-done.4 = bf16[128,512]{1,0:T(8,128)(2,1)S(1)} copy-done((bf16[128,512]{1,0:T(8,128)(2,1)S(1)}, bf16[128,512]{1,0:T(8,128)(2,1)}, u32[]{:S(2)}) %copy-start.4) | copy-done | bytes 131096
  6.0 0.0 copy-start.5
  6.0 0.9 %copy-done.5 = bf16[128,512]{1,0:T(8,128)(2,1)S(1)} copy-done((bf16[128,512]{1,0:T(8,128)(2,1)S(1)}, bf16[128,512]{1,0:T(8,128)(2,1)}, u32[]{:S(2)}) %copy-start.5) | copy-done | bytes 131096
  6.9 0.0 copy-start.6
  6.9 0.7 %copy-done.6 = f32[8,128]{1,0:T(8,128)S(1)} copy-done((f32[8,128]{1,0:T(8,128)S(1)}, f32[8,128]{1,0:T(8,128)}, u32[]{:S(2)}) %copy-start.6) | copy-done | bytes 4120
  7.6 0.0 copy-start.7
  7.6 0.7 %copy-done.7 = f32[8,128]{1,0:T(8,128)S(1)} copy-done((f32[8,128]{1,0:T(8,128)S(1)}, f32[8,128]{1,0:T(8,128)}, u32[]{:S(2)}) %copy-start.7) | copy-done | bytes 4120
  8.3 0.0 copy-start.8
  8.3 0.7 %copy-done.8 = f32[128]{0:T(128)S(1)} copy-done((f32[128]{0:T(128)S(1)}, f32[128]{0:T(128)}, u32[]{:S(2)}) %copy-start.8) | copy-done | bytes 536
  9.0 41.5 %shard_map.91 = bf16[128,512]{1,0:T(8,128)(2,1)S(1)} custom-call(bf16[128,512]{1,0:T(8,128)(2,1)S(1)} %copy-done.4, bf16[128,512]{1,0:T(8,128)(2,1)S(1)} %copy-done.5, bf16[128,1024]{1,0:T(8,128)(2,1)S(1)} %copy-done.2, bf16[128,1024]{1,0:T(8,128)(2,1)S(1)} %copy-done.3, f32[8,128]{1,0:T(8,128)S(1)} %copy-done.6, f32[8,128]{1,0:T(8,128)S(1)} %copy-done.7, ...), custom_call_target="tpu_custom_call" | custom-call | flops 2000000000 | bytes 6000000 | tf_op jit(solution)/shard_map/pallas_call | solution.py:429
  50.5 0.7 %copy.11 = bf16[128,512]{1,0:T(8,128)(2,1)} copy(bf16[128,512]{1,0:T(8,128)(2,1)S(1)} %shard_map.91) | data formatting | bytes 262144
Async XLA Ops:
  0.0 2.2 %copy-start = (bf16[1024,2048]{1,0:T(8,128)(2,1)S(1)}, bf16[1024,2048]{1,0:T(8,128)(2,1)}, u32[]{:S(2)}) copy-start(bf16[1024,2048]{1,0:T(8,128)(2,1)} %weight_hbm.1) | copy-start | bytes 12582916
  2.2 1.0 %copy-start.1 = (f32[8,128,128]{2,1,0:T(8,128)S(1)}, f32[8,128,128]{2,1,0:T(8,128)}, u32[]{:S(2)}) copy-start(f32[8,128,128]{2,1,0:T(8,128)} %init_hbm.1) | copy-start | bytes 1572868
  3.2 0.9 %copy-start.2 = (bf16[128,1024]{1,0:T(8,128)(2,1)S(1)}, bf16[128,1024]{1,0:T(8,128)(2,1)}, u32[]{:S(2)}) copy-start(bf16[128,1024]{1,0:T(8,128)(2,1)} %v_ref.1) | copy-start | bytes 786436
  4.2 0.9 %copy-start.3 = (bf16[128,1024]{1,0:T(8,128)(2,1)S(1)}, bf16[128,1024]{1,0:T(8,128)(2,1)}, u32[]{:S(2)}) copy-start(bf16[128,1024]{1,0:T(8,128)(2,1)} %gate_hbm.1) | copy-start | bytes 786436
  5.1 0.9 %copy-start.4 = (bf16[128,512]{1,0:T(8,128)(2,1)S(1)}, bf16[128,512]{1,0:T(8,128)(2,1)}, u32[]{:S(2)}) copy-start(bf16[128,512]{1,0:T(8,128)(2,1)} %q_ref.1) | copy-start | bytes 393220
  6.0 0.9 %copy-start.5 = (bf16[128,512]{1,0:T(8,128)(2,1)S(1)}, bf16[128,512]{1,0:T(8,128)(2,1)}, u32[]{:S(2)}) copy-start(bf16[128,512]{1,0:T(8,128)(2,1)} %k_ref.1) | copy-start | bytes 393220
  6.9 0.7 %copy-start.6 = (f32[8,128]{1,0:T(8,128)S(1)}, f32[8,128]{1,0:T(8,128)}, u32[]{:S(2)}) copy-start(f32[8,128]{1,0:T(8,128)} %decay_ref.1) | copy-start | bytes 12292
  7.6 0.7 %copy-start.7 = (f32[8,128]{1,0:T(8,128)S(1)}, f32[8,128]{1,0:T(8,128)}, u32[]{:S(2)}) copy-start(f32[8,128]{1,0:T(8,128)} %rate_ref.1) | copy-start | bytes 12292
  8.3 0.7 %copy-start.8 = (f32[128]{0:T(128)S(1)}, f32[128]{0:T(128)}, u32[]{:S(2)}) copy-start(f32[128]{0:T(128)} %param.16) | copy-start | bytes 1540

commit v2 on v1

--- a/solution.py
+++ b/solution.py
@@ -41,18 +41,24 @@
 
 
 def kernel(
+    q_hbm,
+    k_hbm,
+    v_hbm,
+    gate_hbm,
+    decay_hbm,
+    rate_hbm,
+    init_hbm,
+    gain_hbm,
+    weight_hbm,
+    out_ref,
     q_ref,
     k_ref,
     v_ref,
-    gate_hbm,
+    gate_ref,
     decay_ref,
     rate_ref,
-    init_hbm,
+    init_ref,
     gain_ref,
-    weight_hbm,
-    out_ref,
-    gate_ref,
-    init_ref,
     weight_ref,
     wu_ref,
     score_ref,
@@ -100,6 +106,22 @@
             device_id_type=MESH,
         )
 
+    pairs = (
+        (decay_hbm, decay_ref),
+        (rate_hbm, rate_ref),
+        (k_hbm, k_ref),
+        (q_hbm, q_ref),
+        (v_hbm, v_ref),
+        (gate_hbm, gate_ref),
+        (gain_hbm, gain_ref),
+        (init_hbm, init_ref),
+        (weight_hbm, weight_ref),
+    )
+    loads = [
+        pltpu.make_async_copy(src, dst, load_sem.at[i]) for i, (src, dst) in enumerate(pairs)
+    ]
+    for load in loads:
+        load.start()
     barrier = pltpu.get_barrier_semaphore()
     for step in range(1, 16):
         pl.semaphore_signal(
@@ -113,13 +135,6 @@
         pl.semaphore_signal(
             barrier, inc=1, device_id=(seq, lax.rem(y + step, NY)), device_id_type=MESH
         )
-    loads = [
-        pltpu.make_async_copy(init_hbm, init_ref, load_sem.at[0]),
-        pltpu.make_async_copy(gate_hbm, gate_ref, load_sem.at[1]),
-        pltpu.make_async_copy(weight_hbm, weight_ref, load_sem.at[2]),
-    ]
-    for load in loads:
-        load.start()
 
     rows = lax.broadcasted_iota(jnp.int32, (C, C), 0)
     cols = lax.broadcasted_iota(jnp.int32, (C, C), 1)
@@ -128,6 +143,8 @@
     within = rows >= cols
     diagonal = (rows == cols).astype(F32)
     upto = (rows <= cols).astype(BF16)
+    for load in loads[0:5]:
+        load.wait()
     logs = jnp.log(decay_ref[...])
     rates = rate_ref[...]
     high = logs.astype(BF16)
@@ -245,12 +262,11 @@
         pair = mm(score_ref[h], wu_ref[h])
         read_ref[h] = read_ref[h] - pair[:, 0:C]
         local_ref[h] = pair[:, C:]
-    loads[1].wait()
+    for load in loads[5:]:
+        load.wait()
     gate = gate_ref[...].astype(F32)
     gains = jnp.concatenate([gain_ref[...]] * HEADS, axis=1)
     silu_ref[...] = gate / (1.0 + jnp.exp(-gate)) * gains
-    loads[0].wait()
-    loads[2].wait()
 
     works = z // HALF == c
 
@@ -424,16 +440,22 @@
 
 def on_device(q, k, v, gate, decay, rate, init, gain, weight):
     vmem = pl.BlockSpec(memory_space=pltpu.VMEM)
-    anywhere = pl.BlockSpec(memory_space=pl.ANY)
+    hbm = pl.BlockSpec(memory_space=pltpu.HBM)
     dma = pltpu.SemaphoreType.DMA
     return pl.pallas_call(
         kernel,
         out_shape=jax.ShapeDtypeStruct((C, OUT), BF16),
-        in_specs=[vmem, vmem, vmem, anywhere, vmem, vmem, anywhere, vmem, anywhere],
+        in_specs=[hbm] * 9,
         out_specs=vmem,
         scratch_shapes=[
+            pltpu.VMEM((C, KEYS * C), BF16),
+            pltpu.VMEM((C, KEYS * C), BF16),
             pltpu.VMEM((C, HEADS * C), BF16),
+            pltpu.VMEM((C, HEADS * C), BF16),
+            pltpu.VMEM((HEADS, C), F32),
+            pltpu.VMEM((HEADS, C), F32),
             pltpu.VMEM((HEADS, C, C), F32),
+            pltpu.VMEM((1, C), F32),
             pltpu.VMEM((HEADS * C, NY * OUT), BF16),
             pltpu.VMEM((HEADS, C, 2 * C), BF16),
             pltpu.VMEM((HEADS, C, C), BF16),
@@ -454,7 +476,7 @@
             pltpu.VMEM((C, HEADS * C), BF16),
             pltpu.VMEM((NY, C, OUT), BF16),
             pltpu.VMEM((NY, C, OUT), BF16),
-            dma((3,)),
+            dma((9,)),
             dma((HEADS,)),
             dma((HEADS,)),
             dma((HALF,)),
@@ -467,7 +489,7 @@
             dma((NY,)),
         ],
         compiler_params=pltpu.CompilerParams(
-            collective_id=0, has_side_effects=True, vmem_limit_bytes=40 * 2**20
+            collective_id=0, has_side_effects=True, vmem_limit_bytes=62 * 2**20
         ),
         cost_estimate=pl.CostEstimate(
             flops=2 * 10**9, bytes_accessed=6 * 10**6, transcendentals=10**6

time: 51.5 us -> 45 us (0.87)
  local copies, waits for them, and re-layouts: 9.62 us -> 1.57 us
  Pallas kernels: 41.5 us -> 43.3 us
    unnamed x19 -> x1, local copies, waits for them, and re-layouts: 9.62 us -> 1.57 us
    pallas_call x1, Pallas kernels: 41.5 us -> 43.3 us  [on_device(): pl.pallas_call(kernel, out_shape=jax.ShapeDtypeStruct((C, OUT), BF16), in...]
where the time goes in v2:
time: 45 us; the launch traced here: 44.9 us
  Pallas kernels  43.3 us (96%)
  local copies, waits for them, and re-layouts  1.57 us (3%)
    pallas_call x1, Pallas kernels, on_device(): pl.pallas_call(kernel, out_shape=jax.ShapeDtypeStruct((C, OUT), BF16), in...  43.3 us
    unnamed x1, local copies, waits for them, and re-layouts  1.57 us

profile of v2, /device:TPU:199, one launch (start us, length us, event | category | flops | bytes accessed | tf_op | source)
XLA Modules:
  0.0 44.9 jit_solution(10212919938972127192)
XLA Ops:
  0.0 43.3 %shard_map.91 = bf16[128,512]{1,0:T(8,128)(2,1)} custom-call(bf16[128,512]{1,0:T(8,128)(2,1)} %q_hbm.1, bf16[128,512]{1,0:T(8,128)(2,1)} %k_hbm.1, bf16[128,1024]{1,0:T(8,128)(2,1)} %v_hbm.1, bf16[128,1024]{1,0:T(8,128)(2,1)} %gate_hbm.1, f32[8,128]{1,0:T(8,128)} %decay_hbm.1, f32[8,128]{1,0:T(8,128)} %rate_hbm.1, f32[8,128,128]{2,1,0:T(8,128)} %init_hbm.1, ...), custom_call_target="tpu_custom_call" | custom-call | flops 2000000000 | bytes 6000000 | tf_op jit(solution)/shard_map/pallas_call | solution.py:445
  43.3 1.6 %copy.11 = bf16[128,512]{1,0:T(8,128)(2,1)} copy(bf16[128,512]{1,0:T(8,128)(2,1)} %shard_map.91) | data formatting | bytes 262144

commit v3 on v2

--- a/solution.py
+++ b/solution.py
@@ -77,6 +77,8 @@
     give,
     take,
     normed,
+    far,
+    relay,
     part,
     parts,
     load_sem,
@@ -88,6 +90,7 @@
     total_recv,
     give_send,
     take_recv,
+    forward_send,
     part_send,
     parts_recv,
 ):
@@ -262,6 +265,16 @@
         pair = mm(score_ref[h], wu_ref[h])
         read_ref[h] = read_ref[h] - pair[:, 0:C]
         local_ref[h] = pair[:, C:]
+    @pl.when(c == 1)
+    def _():
+        for h in range(HALF):
+            to_other[h].wait_recv()
+        for h in range(HEADS):
+            now = read_ref[h]
+            narrow = now.astype(BF16)
+            read_ref[h] = get_gain(sib, h) * now - mm(narrow, sib[h, 0:C, :])
+            local_ref[h] = local_ref[h] + mm(narrow, sib[h, C : 2 * C, :])
+
     for load in loads[5:]:
         load.wait()
     gate = gate_ref[...].astype(F32)
@@ -280,15 +293,14 @@
             y,
         )
 
-    def to_chip(j, core):
+    def to_chip(j):
         return remote(
-            give.at[j],
-            take.at[z],
-            give_send.at[j * 2 + core],
-            take_recv.at[z],
-            base + j * 2 + core,
-            y,
-        )
+            give.at[j], take.at[z], give_send.at[j], take_recv.at[z], base + j * 2 + c, y
+        )
+
+    def to_sibling(index):
+        h = c * HALF + index
+        return remote(take.at[h], take.at[h], forward_send.at[index], take_recv.at[h], other, y)
 
     @pl.when(works)
     def _():
@@ -351,35 +363,25 @@
         for j in range(NZ):
             here = prefix_g[j][0:1, :] * entry - mm(prefix_d[j], narrow) + prefix_c[j]
             give[j] = here.astype(BF16)
-            for core in range(2):
-
-                @pl.when((z != j) | (c != core))
-                def _():
-                    to_chip(j, core).start()
+
+            @pl.when(z != j)
+            def _():
+                to_chip(j).start()
 
         take[z] = give[z]
 
-    @pl.when(c == 1)
-    def _():
-        for h in range(HALF):
-            to_other[h].wait_recv()
-
-    for h in range(HEADS):
-
-        @pl.when(jnp.logical_not(works) | (z != h))
+    for index in range(HALF):
+        h = c * HALF + index
+
+        @pl.when(z != h)
         def _():
             remote(take.at[h], take.at[h], give_send.at[0], take_recv.at[h], other, y).wait_recv()
 
-        @pl.when(c == 1)
-        def _():
-            now = take[h]
-            here = (
-                get_gain(sib, h) * now.astype(F32)
-                - mm(sib[h, 0:C, :], now)
-                + sib[h, C : 2 * C, :].astype(F32)
-            )
-            take[h] = here.astype(BF16)
-
+        to_sibling(index).start()
+    for index in range(HALF):
+        h = (1 - c) * HALF + index
+        remote(take.at[h], take.at[h], give_send.at[0], take_recv.at[h], other, y).wait_recv()
+    for h in range(HEADS):
         o = mm(read_ref[h].astype(BF16), take[h]) + local_ref[h]
         scale = lax.rsqrt(jnp.sum(o * o, axis=1, keepdims=True) * (1.0 / C) + 1e-6)
         normed[:, h * C : (h + 1) * C] = (o * scale * silu_ref[:, h * C : (h + 1) * C]).astype(BF16)
@@ -387,27 +389,44 @@
     def columns(to_y):
         return weight_ref[:, pl.ds(pl.multiple_of(to_y * OUT, OUT), OUT)]
 
-    def to_row(step):
-        return remote(
-            part.at[step],
-            parts.at[step],
-            part_send.at[step],
-            parts_recv.at[step],
-            seq,
-            lax.rem(y + step, NY),
-        )
-
-    for step in (2, 1, 3):
-        part[step] = mm(normed[...], columns(lax.rem(y + step, NY))).astype(BF16)
-        to_row(step).start()
+    above, below = lax.rem(y + 1, NY), lax.rem(y + NY - 1, NY)
+    upper, lower_half = pl.ds(0, C // 2), pl.ds(C // 2, C // 2)
+
+    def row_copy(src, dst, i, to_y):
+        return remote(src, dst, part_send.at[i], parts_recv.at[i], seq, to_y)
+
+    copies = (
+        row_copy(far.at[upper], relay.at[0], 0, above),
+        row_copy(far.at[lower_half], relay.at[1], 1, below),
+        row_copy(part.at[0, lower_half], parts.at[0, lower_half], 2, above),
+        row_copy(part.at[1, upper], parts.at[1, upper], 3, below),
+        row_copy(part.at[0, upper], parts.at[0, upper], 4, above),
+        row_copy(part.at[1, lower_half], parts.at[1, lower_half], 5, below),
+    )
+    far[...] = mm(normed[...], columns(lax.rem(y + 2, NY))).astype(BF16)
+    copies[0].start()
+    copies[1].start()
+    rising = mm(normed[...], columns(above))
+    part[0, C // 2 :, :] = rising[C // 2 :].astype(BF16)
+    copies[2].start()
+    falling = mm(normed[...], columns(below))
+    part[1, 0 : C // 2, :] = falling[0 : C // 2].astype(BF16)
+    copies[3].start()
+    copies[0].wait_recv()
+    part[0, 0 : C // 2, :] = (rising[0 : C // 2] + relay[0].astype(F32)).astype(BF16)
+    copies[4].start()
+    copies[1].wait_recv()
+    part[1, C // 2 :, :] = (falling[C // 2 :] + relay[1].astype(F32)).astype(BF16)
+    copies[5].start()
     mine = mm(normed[...], columns(y))
-    for step in (1, 3, 2):
-        to_row(step).wait_recv()
-        mine = mine + parts[step].astype(F32)
-    out_ref[...] = mine.astype(BF16)
-
-    for step in (2, 1, 3):
-        to_row(step).wait_send()
+    for i in (2, 3, 4, 5):
+        copies[i].wait_recv()
+    out_ref[...] = (mine + parts[0].astype(F32) + parts[1].astype(F32)).astype(BF16)
+
+    for copy in copies:
+        copy.wait_send()
+    for index in range(HALF):
+        to_sibling(index).wait_send()
     for h in range(HALF):
         to_other[h].wait_send()
 
@@ -431,11 +450,10 @@
                 to_segment(step).wait_send()
 
         for j in range(NZ):
-            for core in range(2):
-
-                @pl.when((z != j) | (c != core))
-                def _():
-                    to_chip(j, core).wait_send()
+
+            @pl.when(z != j)
+            def _():
+                to_chip(j).wait_send()
 
 
 def on_device(q, k, v, gate, decay, rate, init, gain, weight):
@@ -474,8 +492,10 @@
             pltpu.VMEM((NZ, C, C), BF16),
             pltpu.VMEM((HEADS, C, C), BF16),
             pltpu.VMEM((C, HEADS * C), BF16),
-            pltpu.VMEM((NY, C, OUT), BF16),
-            pltpu.VMEM((NY, C, OUT), BF16),
+            pltpu.VMEM((C, OUT), BF16),
+            pltpu.VMEM((2, C // 2, OUT), BF16),
+            pltpu.VMEM((2, C, OUT), BF16),
+            pltpu.VMEM((2, C, OUT), BF16),
             dma((9,)),
             dma((HEADS,)),
             dma((HEADS,)),
@@ -483,10 +503,11 @@
             dma((NZ,)),
             dma((NX,)),
             dma((NX,)),
-            dma((2 * NZ,)),
+            dma((NZ,)),
             dma((HEADS,)),
-            dma((NY,)),
-            dma((NY,)),
+            dma((HALF,)),
+            dma((6,)),
+            dma((6,)),
         ],
         compiler_params=pltpu.CompilerParams(
             collective_id=0, has_side_effects=True, vmem_limit_bytes=62 * 2**20

time: 45 us -> 41 us (0.911)
  the two profiles are of different devices: /device:TPU:199 before, /device:TPU:7 now
where the time goes in v3:
time: 41 us; the launch traced here: 40.9 us
  Pallas kernels  39.3 us (96%)
  local copies, waits for them, and re-layouts  1.57 us (4%)
    pallas_call x1, Pallas kernels, on_device(): pl.pallas_call(kernel, out_shape=jax.ShapeDtypeStruct((C, OUT), BF16), in...  39.3 us
    unnamed x1, local copies, waits for them, and re-layouts  1.57 us

profile of v3, /device:TPU:7, one launch (start us, length us, event | category | flops | bytes accessed | tf_op | source)
XLA Modules:
  0.0 40.9 jit_solution(8909883849992099017)
XLA Ops:
  0.0 39.3 %shard_map.91 = bf16[128,512]{1,0:T(8,128)(2,1)} custom-call(bf16[128,512]{1,0:T(8,128)(2,1)} %q_hbm.1, bf16[128,512]{1,0:T(8,128)(2,1)} %k_hbm.1, bf16[128,1024]{1,0:T(8,128)(2,1)} %v_hbm.1, bf16[128,1024]{1,0:T(8,128)(2,1)} %gate_hbm.1, f32[8,128]{1,0:T(8,128)} %decay_hbm.1, f32[8,128]{1,0:T(8,128)} %rate_hbm.1, f32[8,128,128]{2,1,0:T(8,128)} %init_hbm.1, ...), custom_call_target="tpu_custom_call" | custom-call | flops 2000000000 | bytes 6000000 | tf_op jit(solution)/shard_map/pallas_call | solution.py:463
  39.3 1.6 %copy.11 = bf16[128,512]{1,0:T(8,128)(2,1)} copy(bf16[128,512]{1,0:T(8,128)(2,1)} %shard_map.91) | data formatting | bytes 262144

commit v4 on v3

--- a/solution.py
+++ b/solution.py
@@ -19,6 +19,7 @@
 HALF = HEADS // 2
 MSG = 2 * C + 16
 OUT = 512
+PIECE = 256
 
 
 def mm(a, b):
@@ -61,12 +62,11 @@
     gain_ref,
     weight_ref,
     wu_ref,
-    score_ref,
+    fade_ref,
     read_ref,
     local_ref,
     silu_ref,
-    own,
-    sib,
+    pair,
     comb,
     chain,
     total,
@@ -79,6 +79,8 @@
     normed,
     far,
     relay,
+    plain,
+    plains,
     part,
     parts,
     load_sem,
@@ -113,8 +115,8 @@
         (decay_hbm, decay_ref),
         (rate_hbm, rate_ref),
         (k_hbm, k_ref),
+        (v_hbm, v_ref),
         (q_hbm, q_ref),
-        (v_hbm, v_ref),
         (gate_hbm, gate_ref),
         (gain_hbm, gain_ref),
         (init_hbm, init_ref),
@@ -123,7 +125,7 @@
     loads = [
         pltpu.make_async_copy(src, dst, load_sem.at[i]) for i, (src, dst) in enumerate(pairs)
     ]
-    for load in loads:
+    for load in loads[0:4]:
         load.start()
     barrier = pltpu.get_barrier_semaphore()
     for step in range(1, 16):
@@ -146,7 +148,7 @@
     within = rows >= cols
     diagonal = (rows == cols).astype(F32)
     upto = (rows <= cols).astype(BF16)
-    for load in loads[0:5]:
+    for load in loads[0:3]:
         load.wait()
     logs = jnp.log(decay_ref[...])
     rates = rate_ref[...]
@@ -161,27 +163,24 @@
     lower, inverse, row_keys, col_keys = [], [], [], []
     for kh in range(KEYS):
         keys = k_ref[:, kh * C : (kh + 1) * C]
-        asks = q_ref[:, kh * C : (kh + 1) * C]
         inner = mm_t(keys, keys)
-        cross = mm_t(asks, keys)
         squares = inner * diagonal
         row_key = lax.rsqrt(jnp.sum(squares, axis=0, keepdims=True) + 1e-6)
         col_key = lax.rsqrt(jnp.sum(squares, axis=1, keepdims=True) + 1e-6)
-        wide_asks = asks.astype(F32)
-        col_ask = lax.rsqrt(jnp.sum(wide_asks * wide_asks, axis=1, keepdims=True) + 1e-6)
-        col_ask = col_ask * (C**-0.5)
         row_keys.append(row_key)
         col_keys.append(col_key)
         for h in (2 * kh, 2 * kh + 1):
             cum_col = tall[:, h : h + 1]
             rate_col = tall[:, HEADS + h : HEADS + h + 1]
             fade = jnp.exp(jnp.where(within, cum_col - cum[h : h + 1, :], 0.0))
-            fade = fade * row_key
+            fade = jnp.where(within, fade * row_key, 0.0)
+            fade_ref[h] = fade
             low_part = jnp.where(strict, inner * fade * (rate_col * col_key), 0.0).astype(BF16)
             lower.append(low_part)
-            score_ref[h] = jnp.where(within, cross * fade * col_ask, 0.0).astype(BF16)
-            read_ref[h] = wide_asks * (col_ask * jnp.exp(cum_col))
             inverse.append(jnp.where(apart == 1, -low_part.astype(F32), diagonal).astype(BF16))
+    loads[3].wait()
+    for load in loads[4:]:
+        load.start()
     size = 2
     while size < C:
         mask = ((apart >= size) & (apart < 2 * size)).astype(BF16)
@@ -201,42 +200,43 @@
             wu_ref[h] = both.astype(BF16)
             fade_col = col_keys[kh] * jnp.exp(ends[h] - tall[:, h : h + 1])
             maps = mm(keys_t, (both * fade_col).astype(BF16))
-            own[h, 0:C, :] = maps[:, 0:C].astype(BF16)
-            own[h, C : 2 * C, :] = maps[:, C:].astype(BF16)
-            put_gain(own, h, jnp.exp(ends[h]))
+            pair[c, h, 0:C, :] = maps[:, 0:C].astype(BF16)
+            pair[c, h, C : 2 * C, :] = maps[:, C:].astype(BF16)
+            put_gain(pair.at[c], h, jnp.exp(ends[h]))
 
     pl.semaphore_wait(barrier, 15 + NX - 1 + NY - 1)
 
-    to_other = [
-        remote(own.at[h], sib.at[h], sib_send.at[h], sib_recv.at[h], other, y)
-        for h in range(HEADS)
-    ]
+    def to_other(h):
+        return remote(
+            pair.at[c, h], pair.at[c, h], sib_send.at[h], sib_recv.at[h], other, y
+        )
+
+    def from_other(h):
+        return remote(
+            pair.at[1 - c, h], pair.at[1 - c, h], sib_send.at[h], sib_recv.at[h], other, y
+        )
+
+    for index in range(HALF):
+        to_other((1 - c) * HALF + index).start()
 
     @pl.when(c == 0)
     def _():
-        for h in range(HALF, HEADS):
-            to_other[h].start()
-
-    for h in range(HALF):
-        to_other[h].start()
+        for h in range(HALF):
+            to_other(h).start()
 
     def joined(index):
         h = c * HALF + index
-        remote(own.at[h], sib.at[h], sib_send.at[h], sib_recv.at[h], other, y).wait_recv()
-        mine, theirs = own[h, 0 : 2 * C, :], sib[h, 0 : 2 * C, :]
-        my_gain, their_gain = get_gain(own, h), get_gain(sib, h)
-        first = c == 0
-        early = jnp.where(first, mine.astype(F32), theirs.astype(F32))
-        late = jnp.where(first, theirs.astype(F32), mine.astype(F32))
-        early_gain = jnp.where(first, my_gain, their_gain)
-        late_gain = jnp.where(first, their_gain, my_gain)
-        late_map = late[0:C].astype(BF16)
-        pair = jnp.concatenate([early[0:C], early[C:]], axis=1).astype(BF16)
-        moved = mm(late_map, pair)
+        early, late = pair.at[0], pair.at[1]
+        early_gain, late_gain = get_gain(early, h), get_gain(late, h)
+        early_map, late_map = early[h, 0:C, :], late[h, 0:C, :]
+        early_bias, late_bias = early[h, C : 2 * C, :], late[h, C : 2 * C, :]
+        moved = mm(late_map, jnp.concatenate([early_map, early_bias], axis=1))
         comb[index, 0:C, :] = (
-            late_gain * early[0:C] + early_gain * late[0:C] - moved[:, 0:C]
+            late_gain * early_map.astype(F32) + early_gain * late_map.astype(F32) - moved[:, 0:C]
         ).astype(BF16)
-        comb[index, C : 2 * C, :] = (late_gain * early[C:] + late[C:] - moved[:, C:]).astype(BF16)
+        comb[index, C : 2 * C, :] = (
+            late_gain * early_bias.astype(F32) + late_bias.astype(F32) - moved[:, C:]
+        ).astype(BF16)
         put_gain(comb, index, early_gain * late_gain)
 
     def to_chain(index):
@@ -250,30 +250,43 @@
             y,
         )
 
-    for index in range(HALF):
-        joined(index)
-
-        @pl.when(z != c * HALF + index)
-        def _():
-            to_chain(index).start()
-
-        @pl.when(z == c * HALF + index)
-        def _():
-            chain[z] = comb[index]
-
-    for h in range(HEADS):
-        pair = mm(score_ref[h], wu_ref[h])
-        read_ref[h] = read_ref[h] - pair[:, 0:C]
-        local_ref[h] = pair[:, C:]
+    for group in (0, 2):
+        for index in (group, group + 1):
+            from_other(c * HALF + index).wait_recv()
+        for index in (group, group + 1):
+            joined(index)
+        for index in (group, group + 1):
+
+            @pl.when(z != c * HALF + index)
+            def _():
+                to_chain(index).start()
+
+            @pl.when(z == c * HALF + index)
+            def _():
+                chain[z] = comb[index]
+
+    loads[4].wait()
+    for kh in range(KEYS):
+        keys = k_ref[:, kh * C : (kh + 1) * C]
+        asks = q_ref[:, kh * C : (kh + 1) * C]
+        wide_asks = asks.astype(F32)
+        col_ask = lax.rsqrt(jnp.sum(wide_asks * wide_asks, axis=1, keepdims=True) + 1e-6)
+        col_ask = col_ask * (C**-0.5)
+        cross = mm_t(asks, keys) * col_ask
+        for h in (2 * kh, 2 * kh + 1):
+            both = mm((cross * fade_ref[h]).astype(BF16), wu_ref[h])
+            read_ref[h] = wide_asks * (col_ask * jnp.exp(tall[:, h : h + 1])) - both[:, 0:C]
+            local_ref[h] = both[:, C:]
+
     @pl.when(c == 1)
     def _():
         for h in range(HALF):
-            to_other[h].wait_recv()
+            from_other(h).wait_recv()
         for h in range(HEADS):
             now = read_ref[h]
             narrow = now.astype(BF16)
-            read_ref[h] = get_gain(sib, h) * now - mm(narrow, sib[h, 0:C, :])
-            local_ref[h] = local_ref[h] + mm(narrow, sib[h, C : 2 * C, :])
+            read_ref[h] = get_gain(pair.at[0], h) * now - mm(narrow, pair[0, h, 0:C, :])
+            local_ref[h] = local_ref[h] + mm(narrow, pair[0, h, C : 2 * C, :])
 
     for load in loads[5:]:
         load.wait()
@@ -315,8 +328,8 @@
                     chain.at[j], chain.at[j], comb_send.at[0], chain_recv.at[j], other, y
                 ).wait_recv()
 
-            prefix_d[j] = d_now.astype(BF16)
-            prefix_c[j] = c_now
+            prefix_d[j * C : (j + 1) * C, :] = d_now.astype(BF16)
+            prefix_c[j * C : (j + 1) * C, :] = c_now
             prefix_g[j] = jnp.broadcast_to(g_now, (8, C))
             step_map = chain[j, 0:C, :]
             step_bias = chain[j, C : 2 * C, :].astype(F32)
@@ -332,7 +345,7 @@
         total[x, 0:C, :] = d_now.astype(BF16)
         total[x, C : 2 * C, :] = c_now.astype(BF16)
         put_gain(total, x, g_now)
-        for step in range(1, NX):
+        for step in (2, 1, 3):
 
             @pl.when(x + step < NX)
             def _():
@@ -360,9 +373,12 @@
 
         entry = state[...]
         narrow = entry.astype(BF16)
+        moved = mm(prefix_d[...], narrow)
         for j in range(NZ):
-            here = prefix_g[j][0:1, :] * entry - mm(prefix_d[j], narrow) + prefix_c[j]
+            span = slice(j * C, (j + 1) * C)
+            here = prefix_g[j][0:1, :] * entry - moved[span] + prefix_c[span]
             give[j] = here.astype(BF16)
+        for j in range(NZ):
 
             @pl.when(z != j)
             def _():
@@ -386,54 +402,71 @@
         scale = lax.rsqrt(jnp.sum(o * o, axis=1, keepdims=True) * (1.0 / C) + 1e-6)
         normed[:, h * C : (h + 1) * C] = (o * scale * silu_ref[:, h * C : (h + 1) * C]).astype(BF16)
 
-    def columns(to_y):
-        return weight_ref[:, pl.ds(pl.multiple_of(to_y * OUT, OUT), OUT)]
+    def columns(to_y, start, size):
+        return weight_ref[:, pl.ds(pl.multiple_of(to_y * OUT + start, PIECE), size)]
 
     above, below = lax.rem(y + 1, NY), lax.rem(y + NY - 1, NY)
-    upper, lower_half = pl.ds(0, C // 2), pl.ds(C // 2, C // 2)
+    half = (pl.ds(0, C // 2), pl.ds(C // 2, C // 2))
 
     def row_copy(src, dst, i, to_y):
         return remote(src, dst, part_send.at[i], parts_recv.at[i], seq, to_y)
 
-    copies = (
-        row_copy(far.at[upper], relay.at[0], 0, above),
-        row_copy(far.at[lower_half], relay.at[1], 1, below),
-        row_copy(part.at[0, lower_half], parts.at[0, lower_half], 2, above),
-        row_copy(part.at[1, upper], parts.at[1, upper], 3, below),
-        row_copy(part.at[0, upper], parts.at[0, upper], 4, above),
-        row_copy(part.at[1, lower_half], parts.at[1, lower_half], 5, below),
-    )
-    far[...] = mm(normed[...], columns(lax.rem(y + 2, NY))).astype(BF16)
-    copies[0].start()
-    copies[1].start()
-    rising = mm(normed[...], columns(above))
-    part[0, C // 2 :, :] = rising[C // 2 :].astype(BF16)
-    copies[2].start()
-    falling = mm(normed[...], columns(below))
-    part[1, 0 : C // 2, :] = falling[0 : C // 2].astype(BF16)
-    copies[3].start()
-    copies[0].wait_recv()
-    part[0, 0 : C // 2, :] = (rising[0 : C // 2] + relay[0].astype(F32)).astype(BF16)
-    copies[4].start()
-    copies[1].wait_recv()
-    part[1, C // 2 :, :] = (falling[C // 2 :] + relay[1].astype(F32)).astype(BF16)
-    copies[5].start()
-    mine = mm(normed[...], columns(y))
-    for i in (2, 3, 4, 5):
-        copies[i].wait_recv()
-    out_ref[...] = (mine + parts[0].astype(F32) + parts[1].astype(F32)).astype(BF16)
-
-    for copy in copies:
+    relays, sums, directs = [], [], []
+    for way, to_y in enumerate((above, below)):
+        directs.append(row_copy(plain.at[way], plains.at[way], way, to_y))
+        for n in range(2):
+            relays.append(
+                row_copy(far.at[n, half[way]], relay.at[way, n], 2 + 2 * way + n, to_y)
+            )
+            sums.append(
+                row_copy(part.at[way, n], parts.at[way, n], 6 + 2 * way + n, to_y)
+            )
+    for n in range(2):
+        far[n] = mm(normed[...], columns(lax.rem(y + 2, NY), n * PIECE, PIECE)).astype(BF16)
+        relays[n].start()
+        relays[2 + n].start()
+    totals = []
+    for way, to_y in enumerate((above, below)):
+        whole = mm(normed[...], columns(to_y, 0, OUT))
+        totals.append(whole)
+        first = C // 2 if way == 0 else 0
+        for n in range(2):
+            plain[way, n] = whole[
+                first : first + C // 2, n * PIECE : (n + 1) * PIECE
+            ].astype(BF16)
+        directs[way].start()
+    mine = mm(normed[...], columns(y, 0, OUT))
+    for n in range(2):
+        for way in range(2):
+            first = 0 if way == 0 else C // 2
+            relays[2 * way + n].wait_recv()
+            term = totals[way][first : first + C // 2, n * PIECE : (n + 1) * PIECE]
+            part[way, n] = (term + relay[way, n].astype(F32)).astype(BF16)
+            sums[2 * way + n].start()
+    for copy in directs:
+        copy.wait_recv()
+    for n in range(2):
+        for way in range(2):
+            sums[2 * way + n].wait_recv()
+        span = slice(n * PIECE, (n + 1) * PIECE)
+        out_ref[0 : C // 2, span] = (
+            mine[0 : C // 2, span] + parts[0, n].astype(F32) + plains[1, n].astype(F32)
+        ).astype(BF16)
+        out_ref[C // 2 :, span] = (
+            mine[C // 2 :, span] + plains[0, n].astype(F32) + parts[1, n].astype(F32)
+        ).astype(BF16)
+
+    for copy in relays + directs + sums:
         copy.wait_send()
     for index in range(HALF):
         to_sibling(index).wait_send()
-    for h in range(HALF):
-        to_other[h].wait_send()
+    for index in range(HALF):
+        to_other((1 - c) * HALF + index).wait_send()
 
     @pl.when(c == 0)
     def _():
-        for h in range(HALF, HEADS):
-            to_other[h].wait_send()
+        for h in range(HALF):
+            to_other(h).wait_send()
 
     for index in range(HALF):
 
@@ -449,11 +482,8 @@
             def _():
                 to_segment(step).wait_send()
 
-        for j in range(NZ):
-
-            @pl.when(z != j)
-            def _():
-                to_chip(j).wait_send()
+        for away in range(1, NZ):
+            to_chip(lax.rem(z + away, NZ)).wait_send()
 
 
 def on_device(q, k, v, gate, decay, rate, init, gain, weight):
@@ -476,26 +506,27 @@
             pltpu.VMEM((1, C), F32),
             pltpu.VMEM((HEADS * C, NY * OUT), BF16),
             pltpu.VMEM((HEADS, C, 2 * C), BF16),
-            pltpu.VMEM((HEADS, C, C), BF16),
+            pltpu.VMEM((HEADS, C, C), F32),
             pltpu.VMEM((HEADS, C, C), F32),
             pltpu.VMEM((HEADS, C, C), F32),
             pltpu.VMEM((C, HEADS * C), F32),
-            pltpu.VMEM((HEADS, MSG, C), BF16),
-            pltpu.VMEM((HEADS, MSG, C), BF16),
+            pltpu.VMEM((2, HEADS, MSG, C), BF16),
             pltpu.VMEM((HALF, MSG, C), BF16),
             pltpu.VMEM((NZ, MSG, C), BF16),
             pltpu.VMEM((NX, MSG, C), BF16),
-            pltpu.VMEM((NZ, C, C), BF16),
-            pltpu.VMEM((NZ, C, C), F32),
+            pltpu.VMEM((NZ * C, C), BF16),
+            pltpu.VMEM((NZ * C, C), F32),
             pltpu.VMEM((NZ, 8, C), F32),
             pltpu.VMEM((C, C), F32),
             pltpu.VMEM((NZ, C, C), BF16),
             pltpu.VMEM((HEADS, C, C), BF16),
             pltpu.VMEM((C, HEADS * C), BF16),
-            pltpu.VMEM((C, OUT), BF16),
-            pltpu.VMEM((2, C // 2, OUT), BF16),
-            pltpu.VMEM((2, C, OUT), BF16),
-            pltpu.VMEM((2, C, OUT), BF16),
+            pltpu.VMEM((2, C, PIECE), BF16),
+            pltpu.VMEM((2, 2, C // 2, PIECE), BF16),
+            pltpu.VMEM((2, 2, C // 2, PIECE), BF16),
+            pltpu.VMEM((2, 2, C // 2, PIECE), BF16),
+            pltpu.VMEM((2, 2, C // 2, PIECE), BF16),
+            pltpu.VMEM((2, 2, C // 2, PIECE), BF16),
             dma((9,)),
             dma((HEADS,)),
             dma((HEADS,)),
@@ -506,8 +537,8 @@
             dma((NZ,)),
             dma((HEADS,)),
             dma((HALF,)),
-            dma((6,)),
-            dma((6,)),
+            dma((10,)),
+            dma((10,)),
         ],
         compiler_params=pltpu.CompilerParams(
             collective_id=0, has_side_effects=True, vmem_limit_bytes=62 * 2**20

time: 41 us -> 40.5 us (0.988)
  the two profiles are of different devices: /device:TPU:7 before, /device:TPU:199 now
where the time goes in v4:
time: 40.5 us; the launch traced here: 39.7 us
  Pallas kernels  38.1 us (94%)
  local copies, waits for them, and re-layouts  1.57 us (4%)
    pallas_call x1, Pallas kernels, on_device(): pl.pallas_call(kernel, out_shape=jax.ShapeDtypeStruct((C, OUT), BF16), in...  38.1 us
    unnamed x1, local copies, waits for them, and re-layouts  1.57 us

profile of v4, /device:TPU:199, one launch (start us, length us, event | category | flops | bytes accessed | tf_op | source)
XLA Modules:
  0.0 39.7 jit_solution(5612453817783074125)
XLA Ops:
  0.0 38.1 %shard_map.91 = bf16[128,512]{1,0:T(8,128)(2,1)} custom-call(bf16[128,512]{1,0:T(8,128)(2,1)} %q_hbm.1, bf16[128,512]{1,0:T(8,128)(2,1)} %k_hbm.1, bf16[128,1024]{1,0:T(8,128)(2,1)} %v_hbm.1, bf16[128,1024]{1,0:T(8,128)(2,1)} %gate_hbm.1, f32[8,128]{1,0:T(8,128)} %decay_hbm.1, f32[8,128]{1,0:T(8,128)} %rate_hbm.1, f32[8,128,128]{2,1,0:T(8,128)} %init_hbm.1, ...), custom_call_target="tpu_custom_call" | custom-call | flops 2000000000 | bytes 6000000 | tf_op jit(solution)/shard_map/pallas_call | solution.py:493
  38.2 1.6 %copy.11 = bf16[128,512]{1,0:T(8,128)(2,1)} copy(bf16[128,512]{1,0:T(8,128)(2,1)} %shard_map.91) | data formatting | bytes 262144
